TPU v7x, 512 devices: a whole 4x4x16 slice. The times are simulated.
512 devices in a mesh: row: 32 (over z, core), col: 16 (over x, y).
Axes of the slice: x: 4, y: 4, z: 16, core: 2. Of those that a mesh axis runs over, the one named last changes fastest.
Arguments:
- blocks: bfloat16 [16384, 128, 128], P(('row', 'col')), may hold values from -0.09375 to 0.09375
- block_rows: int32 [16384], P(('row', 'col')), may hold values from 0 to 512, as said below
- block_cols: int32 [16384], P(('row', 'col')), may hold values from 0 to 512, as said below
- start: float32 [64, 65536], P(None, ('row', 'col'))
Outputs:
- basis: float32 [64, 65536], P(None, ('row', 'col'))
- alphas: float32 [3, 64, 64], replicated
- betas: float32 [3, 64, 64], replicated
Inputs may be any that keep to these rules, and one draw needn't show every extreme that they name: For device d the entries d * 32 to (d + 1) * 32 - 1 list its stored blocks first and then empty slots, which hold 512 in both lists. A stored block (i, j) has i <= j, i // 16 equal to the device's row index, j % 16 equal to its col index, and no position is stored twice. The devices of row index 0 fill all 32 slots; block_cols holds 512 exactly where block_rows does. `block_cols`: see block_rows.
All inputs are finite; a program needn't handle non-finite values.
Results may differ from a plain program's by a relative error of at most 0.04.
Values may be sent and summed in bfloat16 or wider, within the bound.
A program may use at most 64 MiB of HBM per device.

v0:
```python
import jax
import jax.numpy as jnp
from jax import lax
from jax.sharding import PartitionSpec as P

ITERS = 3
HIGH = lax.Precision.HIGHEST


def local_inner(left, right):
    return jnp.dot(left, right.T, precision=HIGH)


def factorize(gramian, identity):
    factor_low = jnp.linalg.cholesky(gramian)
    inverse = jax.scipy.linalg.solve_triangular(factor_low, identity, lower=True)
    return (inverse, factor_low)


def shards(blocks, block_rows, block_cols, start):
    row_count = lax.axis_size("row")
    col_count = lax.axis_size("col")
    row_index = lax.axis_index("row")
    vec_width = start.shape[0]
    block_size = start.shape[1]
    columns_all = row_count * col_count * block_size
    identity = jnp.eye(vec_width, dtype=jnp.float32)
    row_target = block_rows - row_index * col_count
    col_target = block_cols // col_count
    hot_rows = row_target[:, None] == jnp.arange(col_count)[None, :]
    hot_cols = col_target[:, None] == jnp.arange(row_count)[None, :]
    gramian = lax.psum(local_inner(start, start), ("row", "col")) / columns_all
    inverse, factor_low = factorize(gramian, identity)
    basis = jnp.dot(inverse, start, precision=HIGH)
    previous = None
    alpha_list = []
    beta_list = []
    for step in range(ITERS):
        rounded = basis.astype(jnp.bfloat16)
        row_stripe = lax.all_gather(rounded, "col", axis=1, tiled=True).reshape(
            vec_width, col_count, block_size
        )
        column_set = lax.all_gather(rounded, "row", axis=1, tiled=True).reshape(
            vec_width, row_count, block_size
        )
        taken_cols = jnp.einsum(
            "kmb,sm->ksb",
            column_set,
            hot_cols.astype(jnp.bfloat16),
            preferred_element_type=jnp.float32,
        ).astype(jnp.bfloat16)
        taken_rows = jnp.einsum(
            "kmb,sm->ksb",
            row_stripe,
            hot_rows.astype(jnp.bfloat16),
            preferred_element_type=jnp.float32,
        ).astype(jnp.bfloat16)
        forward = jnp.einsum("ksb,sdb->ksd", taken_cols, blocks, preferred_element_type=jnp.float32)
        row_part = jnp.einsum("ksd,sm->kmd", forward, hot_rows.astype(jnp.float32), precision=HIGH)
        backward = jnp.einsum(
            "ksb,sbd->ksd", taken_rows, blocks, preferred_element_type=jnp.float32
        )
        col_part = jnp.einsum("ksd,sm->kmd", backward, hot_cols.astype(jnp.float32), precision=HIGH)
        own_rows = lax.psum_scatter(
            row_part.astype(jnp.bfloat16), "col", scatter_dimension=1, tiled=True
        ).astype(jnp.float32)
        own_cols = lax.psum_scatter(
            col_part.astype(jnp.bfloat16), "row", scatter_dimension=1, tiled=True
        ).astype(jnp.float32)
        residue = own_rows.reshape(vec_width, block_size) + own_cols.reshape(vec_width, block_size)
        if previous is not None:
            residue = residue - jnp.dot(factor_low.T, previous, precision=HIGH)
        alpha = lax.psum(local_inner(basis, residue), ("row", "col")) / columns_all
        residue = residue - jnp.dot(alpha.T, basis, precision=HIGH)
        gramian = lax.psum(local_inner(residue, residue), ("row", "col")) / columns_all
        inverse, factor_low = factorize(gramian, identity)
        alpha_list.append(alpha)
        beta_list.append(factor_low)
        previous = basis
        basis = jnp.dot(inverse, residue, precision=HIGH)
    return (basis, jnp.stack(alpha_list), jnp.stack(beta_list))


def solution(mesh):
    in_specs = (
        P(("row", "col"), None, None),
        P(("row", "col")),
        P(("row", "col")),
        P(None, ("row", "col")),
    )
    out_specs = (P(None, ("row", "col")), P(), P())
    return jax.shard_map(shards, mesh=mesh, in_specs=in_specs, out_specs=out_specs, check_vma=False)
```

profile of v0, /device:TPU:1, one launch (start us, length us, event | category | flops | bytes accessed | tf_op | source)
XLA Modules:
  0.0 1513.7 jit_solution(926172588916791671)
XLA Ops:
  8.3 111.2 %psum.49 = f32[64,64]{0,1:T(8,128)S(1)} all-reduce(f32[64,64]{0,1:T(8,128)S(1)} %fusion.127), channel_id=1, replica_groups=mesh['row'=32,'col'=16] {'row','col'}, use_global_device_ids=true, to_apply=%region_0.1 | all-reduce | flops 4096 | bytes 32768 | tf_op jit(solution)/shard_map/psum | solution.py:32
  119.5 5.8 cholesky.74
  126.7 4.9 custom-call.8
  133.2 29.9 %all_gather.18 = bf16[64,4096]{1,0:T(8,128)(2,1)S(1)} all-gather(bf16[64,128]{1,0:T(8,128)(2,1)S(1)} %get-tuple-element.17), channel_id=1, replica_groups=mesh['row'=32,'col'=16] {'row'}, dimensions={1}, use_global_device_ids=true | all-gather | bytes 540672 | tf_op jit(solution)/shard_map/all_gather | solution.py:43
  167.0 16.5 %all_gather.19 = bf16[64,2048]{1,0:T(8,128)(2,1)S(1)} all-gather(bf16[64,128]{1,0:T(8,128)(2,1)S(1)} %get-tuple-element.17), channel_id=1, replica_groups=mesh['row'=32,'col'=16] {'col'}, dimensions={1}, use_global_device_ids=true | all-gather | bytes 278528 | tf_op jit(solution)/shard_map/all_gather | solution.py:40
  184.3 1.3 fusion
  186.6 58.9 %reduce-scatter.19.cloned.1.call-done = bf16[64,1,128]{2,0,1:T(8,128)(2,1)} async-done(((bf16[64,16,128]{2,0,1:T(8,128)(2,1)}), bf16[64,1,128]{2,0,1:T(8,128)(2,1)}) %reduce-scatter.19.cloned.1.call-update) | async-done | bytes 16400
  245.6 108.3 %reduce-scatter.13.cloned.1.call-done = bf16[64,1,128]{2,0,1:T(8,128)(2,1)} async-done(((bf16[64,32,128]{2,0,1:T(8,128)(2,1)}), bf16[64,1,128]{2,0,1:T(8,128)(2,1)}) %reduce-scatter.13.cloned.1.call-update) | async-done | bytes 16400 | tf_op jit(solution)/shard_map/reduce_scatter | solution.py:67
  354.8 106.5 %psum.50 = f32[64,64]{0,1:T(8,128)S(1)} all-reduce(f32[64,64]{0,1:T(8,128)S(1)} %fusion.51), channel_id=1, replica_groups=mesh['row'=32,'col'=16] {'row','col'}, use_global_device_ids=true, to_apply=%region_5.8 | all-reduce | flops 4096 | bytes 32768 | tf_op jit(solution)/shard_map/psum | solution.py:73
  461.7 98.9 %psum.51 = f32[64,64]{0,1:T(8,128)S(1)} all-reduce(f32[64,64]{0,1:T(8,128)S(1)} %fusion.128), channel_id=1, replica_groups=mesh['row'=32,'col'=16] {'row','col'}, use_global_device_ids=true, to_apply=%region_6.9 | all-reduce | flops 4096 | bytes 32768 | tf_op jit(solution)/shard_map/psum | solution.py:75
  560.7 5.8 cholesky.85
  567.9 4.9 custom-call.9
  573.2 31.9 %all_gather.20 = bf16[64,4096]{1,0:T(8,128)(2,1)S(1)} all-gather(bf16[64,128]{1,0:T(8,128)(2,1)S(1)} %get-tuple-element.19), channel_id=1, replica_groups=mesh['row'=32,'col'=16] {'row'}, dimensions={1}, use_global_device_ids=true | all-gather | bytes 540672 | tf_op jit(solution)/shard_map/all_gather | solution.py:43
  605.0 17.4 %all_gather.21 = bf16[64,2048]{1,0:T(8,128)(2,1)S(1)} all-gather(bf16[64,128]{1,0:T(8,128)(2,1)S(1)} %get-tuple-element.19), channel_id=1, replica_groups=mesh['row'=32,'col'=16] {'col'}, dimensions={1}, use_global_device_ids=true | all-gather | bytes 278528 | tf_op jit(solution)/shard_map/all_gather | solution.py:40
  626.5 1.3 fusion.1
  628.8 81.9 %reduce-scatter.21.cloned.1.call-done = bf16[64,1,128]{2,0,1:T(8,128)(2,1)} async-done(((bf16[64,16,128]{2,0,1:T(8,128)(2,1)}), bf16[64,1,128]{2,0,1:T(8,128)(2,1)}) %reduce-scatter.21.cloned.1.call-update) | async-done | bytes 16400
  710.7 108.1 %reduce-scatter.15.cloned.1.call-done = bf16[64,1,128]{2,0,1:T(8,128)(2,1)} async-done(((bf16[64,32,128]{2,0,1:T(8,128)(2,1)}), bf16[64,1,128]{2,0,1:T(8,128)(2,1)}) %reduce-scatter.15.cloned.1.call-update) | async-done | bytes 16400 | tf_op jit(solution)/shard_map/reduce_scatter | solution.py:67
  818.8 1.6 convolution_subtract_fusion.3
  820.7 106.2 %psum.52 = f32[64,64]{0,1:T(8,128)S(1)} all-reduce(f32[64,64]{0,1:T(8,128)S(1)} %fusion.129), channel_id=1, replica_groups=mesh['row'=32,'col'=16] {'row','col'}, use_global_device_ids=true, to_apply=%region_9.12 | all-reduce | flops 4096 | bytes 32768 | tf_op jit(solution)/shard_map/psum | solution.py:73
  927.2 98.9 %psum.53 = f32[64,64]{0,1:T(8,128)S(1)} all-reduce(f32[64,64]{0,1:T(8,128)S(1)} %fusion.130), channel_id=1, replica_groups=mesh['row'=32,'col'=16] {'row','col'}, use_global_device_ids=true, to_apply=%region_10.13 | all-reduce | flops 4096 | bytes 32768 | tf_op jit(solution)/shard_map/psum | solution.py:75
  1026.2 5.8 cholesky.96
  1033.4 4.9 custom-call.10
  1038.7 31.9 %all_gather.22 = bf16[64,4096]{1,0:T(8,128)(2,1)S(1)} all-gather(bf16[64,128]{1,0:T(8,128)(2,1)S(1)} %get-tuple-element.21), channel_id=1, replica_groups=mesh['row'=32,'col'=16] {'row'}, dimensions={1}, use_global_device_ids=true | all-gather | bytes 540672 | tf_op jit(solution)/shard_map/all_gather | solution.py:43
  1070.6 17.6 %all_gather.23 = bf16[64,2048]{1,0:T(8,128)(2,1)S(1)} all-gather(bf16[64,128]{1,0:T(8,128)(2,1)S(1)} %get-tuple-element.21), channel_id=1, replica_groups=mesh['row'=32,'col'=16] {'col'}, dimensions={1}, use_global_device_ids=true | all-gather | bytes 278528 | tf_op jit(solution)/shard_map/all_gather | solution.py:40
  1092.2 1.3 fusion.2
  1094.5 81.9 %reduce-scatter.23.cloned.1.call-done = bf16[64,1,128]{2,0,1:T(8,128)(2,1)} async-done(((bf16[64,16,128]{2,0,1:T(8,128)(2,1)}), bf16[64,1,128]{2,0,1:T(8,128)(2,1)}) %reduce-scatter.23.cloned.1.call-update) | async-done | bytes 16400
  1176.4 108.4 %reduce-scatter.17.cloned.1.call-done = bf16[64,1,128]{2,0,1:T(8,128)(2,1)} async-done(((bf16[64,32,128]{2,0,1:T(8,128)(2,1)}), bf16[64,1,128]{2,0,1:T(8,128)(2,1)}) %reduce-scatter.17.cloned.1.call-update) | async-done | bytes 16400 | tf_op jit(solution)/shard_map/reduce_scatter | solution.py:67
  1284.9 1.6 convolution_subtract_fusion.1
  1286.7 106.3 %psum.54 = f32[64,64]{0,1:T(8,128)S(1)} all-reduce(f32[64,64]{0,1:T(8,128)S(1)} %fusion.131), channel_id=1, replica_groups=mesh['row'=32,'col'=16] {'row','col'}, use_global_device_ids=true, to_apply=%region_13.16 | all-reduce | flops 4096 | bytes 32768 | tf_op jit(solution)/shard_map/psum | solution.py:73
  1393.3 98.9 %psum.55 = f32[64,64]{0,1:T(8,128)S(1)} all-reduce(f32[64,64]{0,1:T(8,128)S(1)} %fusion.132), channel_id=1, replica_groups=mesh['row'=32,'col'=16] {'row','col'}, use_global_device_ids=true, to_apply=%region_14.17 | all-reduce | flops 4096 | bytes 32768 | tf_op jit(solution)/shard_map/psum | solution.py:75
  1492.3 5.8 cholesky.107
  1500.3 4.9 custom-call.11
  (101 shorter events, 29.5 us)
Async XLA Ops:
  7.2 157.0 %copy-start = (bf16[32,128,128]{2,1,0:T(8,128)(2,1)S(1)}, bf16[32,128,128]{2,1,0:T(8,128)(2,1)}, u32[]{:S(2)}) copy-start(bf16[32,128,128]{2,1,0:T(8,128)(2,1)} %param.7) | copy-start | bytes 3145732
  7.2 238.4 %reduce-scatter.19.cloned.1.call-start = ((), (), s32[]{:S(2)}) async-start(), calls=%async_computation.9 | async-start | bytes 278528
  131.6 0.8 copy-start.1
  132.6 0.7 copy-start.4
  163.2 0.7 copy-start.5
  166.9 187.0 %reduce-scatter.13.cloned.1.call-start = ((), (), s32[]{:S(2)}) async-start(), calls=%async_computation.6 | async-start | bytes 540672 | tf_op jit(solution)/shard_map/reduce_scatter | solution.py:67
  186.6 524.1 %reduce-scatter.21.cloned.1.call-start = ((), (), s32[]{:S(2)}) async-start(), calls=%async_computation.10 | async-start | bytes 278528
  354.8 106.5 %copy-start.2 = (bf16[64,1,128]{2,0,1:T(8,128)(2,1)S(1)}, bf16[64,1,128]{2,0,1:T(8,128)(2,1)}, u32[]{:S(2)}) copy-start(bf16[64,1,128]{2,0,1:T(8,128)(2,1)} %reduce-scatter.19.cloned.1.call-done) | copy-start | bytes 49156
  354.8 106.5 %copy-start.3 = (bf16[64,1,128]{2,0,1:T(8,128)(2,1)S(1)}, bf16[64,1,128]{2,0,1:T(8,128)(2,1)}, u32[]{:S(2)}) copy-start(bf16[64,1,128]{2,0,1:T(8,128)(2,1)} %reduce-scatter.13.cloned.1.call-done) | copy-start | bytes 49156
  625.6 193.2 %reduce-scatter.15.cloned.1.call-start = ((), (), s32[]{:S(2)}) async-start(), calls=%async_computation.7 | async-start | bytes 540672 | tf_op jit(solution)/shard_map/reduce_scatter | solution.py:67
  628.8 547.7 %reduce-scatter.23.cloned.1.call-start = ((), (), s32[]{:S(2)}) async-start(), calls=%async_computation.11 | async-start | bytes 278528
  1091.4 193.5 %reduce-scatter.17.cloned.1.call-start = ((), (), s32[]{:S(2)}) async-start(), calls=%async_computation.8 | async-start | bytes 540672 | tf_op jit(solution)/shard_map/reduce_scatter | solution.py:67
Sparse Core Ops, SparseCore 0:
  167.0 78.5 reduce-scatter.18
  248.6 105.2 reduce-scatter.12
  625.8 84.9 reduce-scatter.20
  713.6 105.2 reduce-scatter.14
  1091.5 84.9 reduce-scatter.22
  1179.3 105.5 reduce-scatter.16
where the time goes:
time: 1520 us; the launch traced here: 1510 us
  blocking collectives  872 us (57%)
  waiting for transfers between devices  548 us (36%)
  other arithmetic  49 us (3%)
  matrix products  21.6 us (1%)
    reduce_scatter x3, waiting for transfers between devices, shards(): lax.psum_scatter(col_part.astype(jnp.bfloat16), 'row', scatter_dimension=...  325 us
    psum x3, blocking collectives, shards(): alpha = lax.psum(local_inner(basis, residue), ('row', 'col')) / columns_all  319 us
    psum x3, blocking collectives, shards(): lax.psum(local_inner(residue, residue), ('row', 'col')) / columns_all  297 us
    unnamed x9, waiting for transfers between devices  223 us
    psum x1, blocking collectives, shards(): gramian = lax.psum(local_inner(start, start), ('row', 'col')) / columns_all  111 us
    all_gather x3, blocking collectives, shards(): lax.all_gather(rounded, 'row', axis=1, tiled=True)  93.6 us
    all_gather x3, blocking collectives, shards(): lax.all_gather(rounded, 'col', axis=1, tiled=True)  51.5 us
  transfers between devices with their start and end apart: 6, of which 6 were waited for; matrix products, arithmetic and copies ran while one was open for 1% of the time, Pallas kernels for 0%

commit v1 on v0

--- a/solution.py
+++ b/solution.py
@@ -70,7 +70,10 @@
         residue = own_rows.reshape(vec_width, block_size) + own_cols.reshape(vec_width, block_size)
         if previous is not None:
             residue = residue - jnp.dot(factor_low.T, previous, precision=HIGH)
-        alpha = lax.psum(local_inner(basis, residue), ("row", "col")) / columns_all
+        alpha = (
+            jnp.sum(lax.all_gather(local_inner(basis, residue), ("row", "col")), axis=0)
+            / columns_all
+        )
         residue = residue - jnp.dot(alpha.T, basis, precision=HIGH)
         gramian = lax.psum(local_inner(residue, residue), ("row", "col")) / columns_all
         inverse, factor_low = factorize(gramian, identity)

time: 1520 us -> 1890 us (1.24)
  waiting for transfers between devices: 548 us -> 1210 us
  blocking collectives: 872 us -> 567 us
  other arithmetic: 49 us -> 71.2 us
    all_gather x0 -> x3, waiting for transfers between devices: none -> 671 us  [shards(): lax.all_gather(local_inner(basis, residue), ('row', 'col'))]
    psum x3 -> x0, blocking collectives: 319 us -> none  [shards(): alpha = lax.psum(local_inner(basis, residue), ('row', 'col')) / columns_all]
    reduce_sum x0 -> x3, other arithmetic: none -> 20.8 us  [shards(): jnp.sum(lax.all_gather(local_inner(basis, residue), ('row', 'col')), axis=0)]
    unnamed x9 -> x12, waiting for transfers between devices: 223 us -> 213 us
  transfers between devices with their start and end apart: 6 -> 9, of which waited for: 6 -> 9; matrix products, arithmetic and copies ran while one was open for 1% -> 0% of each run, Pallas kernels for 0% -> 0%
where the time goes in v1:
time: 1890 us
  waiting for transfers between devices  1210 us (64%)
  blocking collectives  567 us (30%)
  other arithmetic  71.2 us (4%)
  matrix products  24.3 us (1%)
    all_gather x3, waiting for transfers between devices, shards(): lax.all_gather(local_inner(basis, residue), ('row', 'col'))  671 us
    reduce_scatter x3, waiting for transfers between devices, shards(): lax.psum_scatter(col_part.astype(jnp.bfloat16), 'row', scatter_dimension=...  325 us
    psum x3, blocking collectives, shards(): lax.psum(local_inner(residue, residue), ('row', 'col')) / columns_all  305 us
    unnamed x12, waiting for transfers between devices  213 us
    psum x1, blocking collectives, shards(): gramian = lax.psum(local_inner(start, start), ('row', 'col')) / columns_all  111 us
    all_gather x3, blocking collectives, shards(): lax.all_gather(rounded, 'row', axis=1, tiled=True)  99.5 us
    all_gather x3, blocking collectives, shards(): lax.all_gather(rounded, 'col', axis=1, tiled=True)  52 us
  transfers between devices with their start and end apart: 9, of which 9 were waited for; matrix products, arithmetic and copies ran while one was open for 0% of the time, Pallas kernels for 0%

profile of v1, /device:TPU:1, one launch (start us, length us, event | category | flops | bytes accessed | tf_op | source)
XLA Modules:
  0.0 1893.2 jit_solution(10752745426983985636)
XLA Ops:
  9.0 111.2 %psum.28 = f32[64,64]{0,1:T(8,128)S(1)} all-reduce(f32[64,64]{0,1:T(8,128)S(1)} %fusion.127), channel_id=1, replica_groups=mesh['row'=32,'col'=16] {'row','col'}, use_global_device_ids=true, to_apply=%region_0.1 | all-reduce | flops 4096 | bytes 32768 | tf_op jit(solution)/shard_map/psum | solution.py:32
  120.2 5.8 cholesky.74
  127.4 4.9 custom-call.8
  133.5 29.9 %all_gather.36 = bf16[64,4096]{1,0:T(8,128)(2,1)S(1)} all-gather(bf16[64,128]{1,0:T(8,128)(2,1)S(1)} %get-tuple-element.17), channel_id=1, replica_groups=mesh['row'=32,'col'=16] {'row'}, dimensions={1}, use_global_device_ids=true | all-gather | bytes 540672 | tf_op jit(solution)/shard_map/all_gather | solution.py:43
  167.3 16.5 all_gather.37
  186.9 59.0 %reduce-scatter.19.cloned.1.call-done = bf16[64,1,128]{2,0,1:T(8,128)(2,1)} async-done(((bf16[64,16,128]{2,0,1:T(8,128)(2,1)}), bf16[64,1,128]{2,0,1:T(8,128)(2,1)}) %reduce-scatter.19.cloned.1.call-update) | async-done | bytes 16400
  245.9 108.7 %reduce-scatter.13.cloned.1.call-done = bf16[64,1,128]{2,0,1:T(8,128)(2,1)} async-done(((bf16[64,32,128]{2,0,1:T(8,128)(2,1)}), bf16[64,1,128]{2,0,1:T(8,128)(2,1)}) %reduce-scatter.13.cloned.1.call-update) | async-done | bytes 16400 | tf_op jit(solution)/shard_map/reduce_scatter | solution.py:67
  356.2 223.8 %all-gather.7.cloned.1.call-done = f32[32768,64]{1,0:T(8,128)} async-done(((f32[64,64]{1,0:T(8,128)}), f32[32768,64]{1,0:T(8,128)}) %all-gather.7.cloned.1.call-update) | async-done | bytes 8388624 | tf_op jit(solution)/shard_map/all_gather | solution.py:74
  580.0 6.9 reduce_sum.27
  587.4 101.5 %psum.29 = f32[64,64]{0,1:T(8,128)S(1)} all-reduce(f32[64,64]{0,1:T(8,128)S(1)} %fusion.128), channel_id=1, replica_groups=mesh['row'=32,'col'=16] {'row','col'}, use_global_device_ids=true, to_apply=%region_6.9 | all-reduce | flops 4096 | bytes 32768 | tf_op jit(solution)/shard_map/psum | solution.py:78
  689.1 5.8 cholesky.85
  696.3 4.9 custom-call.9
  701.6 17.8 all_gather.41
  719.4 34.8 %all_gather.40 = bf16[64,4096]{1,0:T(8,128)(2,1)S(1)} all-gather(bf16[64,128]{1,0:T(8,128)(2,1)S(1)} %get-tuple-element.19), channel_id=1, replica_groups=mesh['row'=32,'col'=16] {'row'}, dimensions={1}, use_global_device_ids=true | all-gather | bytes 540672 | tf_op jit(solution)/shard_map/all_gather | solution.py:43
  760.5 76.8 %reduce-scatter.21.cloned.1.call-done = bf16[64,1,128]{2,0,1:T(8,128)(2,1)} async-done(((bf16[64,16,128]{2,0,1:T(8,128)(2,1)}), bf16[64,1,128]{2,0,1:T(8,128)(2,1)}) %reduce-scatter.21.cloned.1.call-update) | async-done | bytes 16400
  837.3 108.1 %reduce-scatter.15.cloned.1.call-done = bf16[64,1,128]{2,0,1:T(8,128)(2,1)} async-done(((bf16[64,32,128]{2,0,1:T(8,128)(2,1)}), bf16[64,1,128]{2,0,1:T(8,128)(2,1)}) %reduce-scatter.15.cloned.1.call-update) | async-done | bytes 16400 | tf_op jit(solution)/shard_map/reduce_scatter | solution.py:67
  945.4 1.6 convolution_subtract_fusion.3
  947.9 223.5 %all-gather.9.cloned.1.call-done = f32[32768,64]{1,0:T(8,128)} async-done(((f32[64,64]{1,0:T(8,128)}), f32[32768,64]{1,0:T(8,128)}) %all-gather.9.cloned.1.call-update) | async-done | bytes 8388624 | tf_op jit(solution)/shard_map/all_gather | solution.py:74
  1171.4 6.9 reduce_sum.28
  1178.8 101.6 %psum.30 = f32[64,64]{0,1:T(8,128)S(1)} all-reduce(f32[64,64]{0,1:T(8,128)S(1)} %fusion.130), channel_id=1, replica_groups=mesh['row'=32,'col'=16] {'row','col'}, use_global_device_ids=true, to_apply=%region_10.13 | all-reduce | flops 4096 | bytes 32768 | tf_op jit(solution)/shard_map/psum | solution.py:78
  1280.4 5.8 cholesky.96
  1287.6 4.9 custom-call.10
  1293.0 17.8 all_gather.45
  1310.7 34.8 %all_gather.44 = bf16[64,4096]{1,0:T(8,128)(2,1)S(1)} all-gather(bf16[64,128]{1,0:T(8,128)(2,1)S(1)} %get-tuple-element.21), channel_id=1, replica_groups=mesh['row'=32,'col'=16] {'row'}, dimensions={1}, use_global_device_ids=true | all-gather | bytes 540672 | tf_op jit(solution)/shard_map/all_gather | solution.py:43
  1351.9 76.8 %reduce-scatter.23.cloned.1.call-done = bf16[64,1,128]{2,0,1:T(8,128)(2,1)} async-done(((bf16[64,16,128]{2,0,1:T(8,128)(2,1)}), bf16[64,1,128]{2,0,1:T(8,128)(2,1)}) %reduce-scatter.23.cloned.1.call-update) | async-done | bytes 16400
  1428.7 108.2 %reduce-scatter.17.cloned.1.call-done = bf16[64,1,128]{2,0,1:T(8,128)(2,1)} async-done(((bf16[64,32,128]{2,0,1:T(8,128)(2,1)}), bf16[64,1,128]{2,0,1:T(8,128)(2,1)}) %reduce-scatter.17.cloned.1.call-update) | async-done | bytes 16400 | tf_op jit(solution)/shard_map/reduce_scatter | solution.py:67
  1536.9 1.6 convolution_subtract_fusion.1
  1539.4 223.7 %all-gather.11.cloned.1.call-done = f32[32768,64]{1,0:T(8,128)} async-done(((f32[64,64]{1,0:T(8,128)}), f32[32768,64]{1,0:T(8,128)}) %all-gather.11.cloned.1.call-update) | async-done | bytes 8388624 | tf_op jit(solution)/shard_map/all_gather | solution.py:74
  1763.0 6.9 reduce_sum.29
  1771.2 101.6 %psum.31 = f32[64,64]{0,1:T(8,128)S(1)} all-reduce(f32[64,64]{0,1:T(8,128)S(1)} %fusion.132), channel_id=1, replica_groups=mesh['row'=32,'col'=16] {'row','col'}, use_global_device_ids=true, to_apply=%region_14.17 | all-reduce | flops 4096 | bytes 32768 | tf_op jit(solution)/shard_map/psum | solution.py:78
  1872.9 5.8 cholesky.107
  1880.1 4.9 custom-call.11
  (107 shorter events, 36.0 us)
Async XLA Ops:
  7.2 157.3 %copy-start = (bf16[32,128,128]{2,1,0:T(8,128)(2,1)S(1)}, bf16[32,128,128]{2,1,0:T(8,128)(2,1)}, u32[]{:S(2)}) copy-start(bf16[32,128,128]{2,1,0:T(8,128)(2,1)} %param.7) | copy-start | bytes 3145732
  7.2 238.7 %reduce-scatter.19.cloned.1.call-start = ((), (), s32[]{:S(2)}) async-start(), calls=%async_computation.12 | async-start | bytes 278528
  167.2 187.4 %reduce-scatter.13.cloned.1.call-start = ((), (), s32[]{:S(2)}) async-start(), calls=%async_computation.6 | async-start | bytes 540672 | tf_op jit(solution)/shard_map/reduce_scatter | solution.py:67
  186.8 393.2 %all-gather.7.cloned.1.call-start = ((), (), s32[]{:S(2)}) async-start(), calls=%async_computation.9 | async-start | bytes 16809984 | tf_op jit(solution)/shard_map/all_gather | solution.py:74
  245.9 341.2 %copy-start.1 = (bf16[64,1,128]{2,0,1:T(8,128)(2,1)S(1)}, bf16[64,1,128]{2,0,1:T(8,128)(2,1)}, u32[]{:S(2)}) copy-start(bf16[64,1,128]{2,0,1:T(8,128)(2,1)} %reduce-scatter.19.cloned.1.call-done) | copy-start | bytes 49156
  354.6 232.5 %copy-start.2 = (bf16[64,1,128]{2,0,1:T(8,128)(2,1)S(1)}, bf16[64,1,128]{2,0,1:T(8,128)(2,1)}, u32[]{:S(2)}) copy-start(bf16[64,1,128]{2,0,1:T(8,128)(2,1)} %reduce-scatter.13.cloned.1.call-done) | copy-start | bytes 49156
  356.2 481.1 %reduce-scatter.21.cloned.1.call-start = ((), (), s32[]{:S(2)}) async-start(), calls=%async_computation.13 | async-start | bytes 278528
  757.7 187.7 %reduce-scatter.15.cloned.1.call-start = ((), (), s32[]{:S(2)}) async-start(), calls=%async_computation.7 | async-start | bytes 540672 | tf_op jit(solution)/shard_map/reduce_scatter | solution.py:67
  760.5 410.9 %all-gather.9.cloned.1.call-start = ((), (), s32[]{:S(2)}) async-start(), calls=%async_computation.10 | async-start | bytes 16809984 | tf_op jit(solution)/shard_map/all_gather | solution.py:74
  947.8 480.8 %reduce-scatter.23.cloned.1.call-start = ((), (), s32[]{:S(2)}) async-start(), calls=%async_computation.14 | async-start | bytes 278528
  1349.1 187.8 %reduce-scatter.17.cloned.1.call-start = ((), (), s32[]{:S(2)}) async-start(), calls=%async_computation.8 | async-start | bytes 540672 | tf_op jit(solution)/shard_map/reduce_scatter | solution.py:67
  1351.8 411.2 %all-gather.11.cloned.1.call-start = ((), (), s32[]{:S(2)}) async-start(), calls=%async_computation.11 | async-start | bytes 16809984 | tf_op jit(solution)/shard_map/all_gather | solution.py:74
Sparse Core Ops, SparseCore 0:
  167.3 78.5 reduce-scatter.18
  248.9 105.6 reduce-scatter.12
  359.6 220.4 all-gather.6
  757.8 79.3 reduce-scatter.20
  840.1 105.2 reduce-scatter.14
  950.3 221.0 all-gather.8
  1349.2 79.4 reduce-scatter.22
  1431.7 105.1 reduce-scatter.16
  1541.9 221.0 all-gather.10
